TPU v7x, 256 devices: a whole 4x4x8 slice. The times are simulated.
256 devices in a mesh: cuts: 32 (over z, y_hi, core), col: 8 (over y_lo, x).
Axes of the slice: x: 4, y: 4 (y_hi: 2, y_lo: 2; y = y_hi * 2 + y_lo), z: 8, core: 2. Of those that a mesh axis runs over, the one named last changes fastest.
Arguments:
- lower: bfloat16 [16, 32, 512, 512], P('col', 'cuts'), may hold values from -0.109375 to 0.109375
- upper: bfloat16 [16, 32, 512, 512], P('col', 'cuts'), may hold values from -0.109375 to 0.109375
- rhs: bfloat16 [16, 32, 512, 512], P('col', 'cuts'), may hold values from -6 to 6
Outputs:
- reduced: float32 [16, 32, 512, 512], P('col', 'cuts')
All inputs are finite; a program needn't handle non-finite values.
Results may differ from a plain program's by a relative error of at most 0.0051.
Values may be sent and summed in bfloat16 or wider, within the bound.
A program may use at most 128 MiB of HBM per device.

v0:
```python
import jax
import jax.numpy as jnp
from jax import lax
from jax.sharding import PartitionSpec as P

ROWS = 16


def from_behind(value, axis, steps):
    count = lax.axis_size(axis)
    leading, last = (max(0, -steps), min(count, count - steps))
    return lax.ppermute(value, axis, [(source, source + steps) for source in range(leading, last)])


def from_behind_2(block, axis, distance):
    devices = range(lax.axis_size(axis))
    route = [((i - distance) % len(devices), i) for i in devices]
    return lax.ppermute(block, axis, route)


def batch_product(left, right):
    return jnp.einsum("rij,rjk->rik", left, right, preferred_element_type=jnp.float32)


def pair_product(left, right):
    return jnp.einsum("rij,rsjk->rsik", left, right, preferred_element_type=jnp.float32)


def horner(correction, values, product):
    first = (values + product(correction, values)).astype(jnp.bfloat16)
    second = (values + product(correction, first)).astype(jnp.bfloat16)
    return values + product(correction, second)


def settle_down(received, shift_by, lane_index):
    carried = from_behind((received[0][-1:], received[1][-1:]), "col", 1)
    wrapped = lane_index < shift_by
    first = jnp.where(wrapped, jnp.concatenate([carried[0], received[0][:-1]], axis=0), received[0])
    second = jnp.where(
        wrapped, jnp.concatenate([carried[1], received[1][:-1]], axis=0), received[1]
    )
    return (first, second)


def settle_up(received, shift_by, lane_index, lane_count):
    carried = from_behind((received[0][:1], received[1][:1]), "col", -1)
    wrapped = lane_index >= lane_count - shift_by
    first = jnp.where(wrapped, jnp.concatenate([received[0][1:], carried[0]], axis=0), received[0])
    second = jnp.where(wrapped, jnp.concatenate([received[1][1:], carried[1]], axis=0), received[1])
    return (first, second)


def on_device(lower, upper, rhs):
    lane_count = lax.axis_size("cuts")
    lane_index = lax.axis_index("cuts")
    column_index = lax.axis_index("col")
    lower_blocks = lower[:, 0]
    upper_blocks = upper[:, 0]
    right_side = rhs[:, 0]
    total_rows = ROWS
    first_row = column_index * lower_blocks.shape[0]
    local_rows = lower_blocks.shape[0]
    row_ids = first_row + jnp.arange(local_rows, dtype=jnp.int32)
    slice_ids = row_ids * lane_count + lane_index
    keep_lower = (slice_ids != 0)[:, None, None]
    keep_upper = (slice_ids != total_rows * lane_count - 1)[:, None, None]
    lower_blocks = jnp.where(keep_lower, lower_blocks, jnp.zeros_like(lower_blocks))
    upper_blocks = jnp.where(keep_upper, upper_blocks, jnp.zeros_like(upper_blocks))
    blocks = jnp.stack([lower_blocks, upper_blocks], axis=1)
    below = from_behind_2((blocks, right_side), "cuts", 1)
    below_blocks, below_right = settle_down(below, 1, lane_index)
    above = from_behind_2((blocks, right_side), "cuts", -1)
    above_blocks, above_right = settle_up(above, 1, lane_index, lane_count)
    lower_piece = blocks[:, 0]
    upper_piece = blocks[:, 1]
    correction = batch_product(lower_piece, below_blocks[:, 1]) + batch_product(
        upper_piece, above_blocks[:, 0]
    )
    lower_sum = batch_product(lower_piece, below_blocks[:, 0])
    upper_sum = batch_product(upper_piece, above_blocks[:, 1])
    source = batch_product(lower_piece, below_right) + batch_product(upper_piece, above_right)
    correction, lower_sum, upper_sum, source = (correction, lower_sum, upper_sum, source)
    correction = correction.astype(jnp.bfloat16)
    whole_correction = correction
    terms = jnp.stack(
        [(-lower_sum).astype(jnp.bfloat16), (-upper_sum).astype(jnp.bfloat16)], axis=1
    )
    source = (right_side - source).astype(jnp.bfloat16)
    blocks_one = horner(whole_correction, terms, pair_product).astype(jnp.bfloat16)
    right_one = horner(whole_correction, source, batch_product).astype(jnp.bfloat16)
    below_two = from_behind_2((blocks_one[:, 1], right_one), "cuts", 2)
    below_upper, below_right = settle_down(below_two, 2, lane_index)
    above_two = from_behind_2((blocks_one[:, 0], right_one), "cuts", -2)
    above_lower, above_right = settle_up(above_two, 2, lane_index, lane_count)
    lower_piece = blocks_one[:, 0]
    upper_piece = blocks_one[:, 1]
    correction = batch_product(lower_piece, below_upper) + batch_product(upper_piece, above_lower)
    source = batch_product(lower_piece, below_right) + batch_product(upper_piece, above_right)
    correction_two = correction
    source_two = source
    correction_two = correction_two.astype(jnp.bfloat16)
    source_two = (right_one - source_two).astype(jnp.bfloat16)
    result = horner(correction_two, source_two, batch_product)
    return result[:, None]


def solution(mesh):
    return jax.shard_map(
        on_device,
        mesh=mesh,
        in_specs=(
            P("col", "cuts", None, None),
            P("col", "cuts", None, None),
            P("col", "cuts", None, None),
        ),
        out_specs=P("col", "cuts", None, None),
        check_vma=False,
    )
```

profile of v0, /device:TPU:174, one launch (start us, length us, event | category | flops | bytes accessed | tf_op | source)
XLA Modules:
  0.0 293.8 jit_solution(10993441603161140740)
XLA Ops:
  0.0 1.5 bitcast_select_fusion
  1.7 1.5 pad_maximum_fusion
  3.2 2.2 collective-permute-start.6
  5.4 0.7 collective-permute-start.2
  6.0 0.9 collective-permute-start
  6.9 33.6 %collective-permute-done.2 = bf16[2,512,512]{2,1,0:T(8,128)(2,1)} collective-permute-done((bf16[2,512,512]{2,1,0:T(8,128)(2,1)}, bf16[2,512,512]{2,1,0:T(8,128)(2,1)}, u32[]{:S(2)}, u32[]{:S(2)}) %collective-permute-start.2) | collective-permute-done | bytes 1048608 | tf_op jit(solution)/shard_map/ppermute | solution.py:18
  40.5 1.3 fusion.51
  41.8 2.8 collective-permute-start.3
  44.6 1.0 collective-permute-done
  45.6 1.3 fusion.50
  46.8 1.4 collective-permute-start.1
  48.3 1.7 fusion.45
  50.0 4.6 %collective-permute-start.7 = (bf16[1,2,512,512]{3,2,0,1:T(8,128)(2,1)S(1)}, bf16[1,2,512,512]{3,2,0,1:T(8,128)(2,1)S(1)}, u32[]{:S(2)}, u32[]{:S(2)}) collective-permute-start(bf16[1,2,512,512]{3,2,0,1:T(8,128)(2,1)S(1)} %get-tuple-element.10), channel_id=1, source_target_pairs={{1,0},{2,1},{3,2},{4,3},{5,4},{6,5},{7,6},{9,8},{10,9},{11,10},{12... | collective-permute-start | bytes 3145736 | tf_op jit(solution)/shard_map/ppermute | solution.py:12
  54.7 2.0 fusion.14
  56.8 1.3 collective-permute-start.5
  58.1 3.4 %subtract_convert_fusion.1 = bf16[2,512,512]{2,1,0:T(8,128)(2,1)} fusion(f32[2,512,512]{2,1,0:T(8,128)S(1)} %fusion.14, bf16[2,512,512]{2,1,0:T(8,128)(2,1)} %collective-permute-done, bf16[1,512,512]{2,1,0:T(8,128)(2,1)S(1)} %get-tuple-element.20, bf16[1,512,512]{2,1,0:T(8,128)(2,1)S(1)} %collective-permute-done.1, pred[]{:T(512)S(6)} %lt.6, ...), kind=kOutput, calls=%fused_computation.27 | convolution fusion | flops 540540928 | bytes 7340035 | tf_op jit(solution)/shard_map/rij,rjk->rik/dot_general | solution.py:22
  61.5 5.4 %collective-permute-done.7 = bf16[1,2,512,512]{3,2,0,1:T(8,128)(2,1)S(1)} collective-permute-done((bf16[1,2,512,512]{3,2,0,1:T(8,128)(2,1)S(1)}, bf16[1,2,512,512]{3,2,0,1:T(8,128)(2,1)S(1)}, u32[]{:S(2)}, u32[]{:S(2)}) %collective-permute-start.7) | collective-permute-done | bytes 1048608 | tf_op jit(solution)/shard_map/ppermute | solution.py:12
  66.9 1.9 maximum_select_fusion.1
  68.7 0.8 fusion.10
  69.5 0.7 fusion.11
  70.3 3.3 %collective-permute-done.5 = bf16[1,2,512,512]{3,2,0,1:T(8,128)(2,1)S(1)} collective-permute-done((bf16[1,2,512,512]{3,2,0,1:T(8,128)(2,1)S(1)}, bf16[1,2,512,512]{3,2,0,1:T(8,128)(2,1)S(1)}, u32[]{:S(2)}, u32[]{:S(2)}) %collective-permute-start.5) | collective-permute-done | bytes 1048608 | tf_op jit(solution)/shard_map/ppermute | solution.py:12
  73.5 0.3 maximum_select_fusion
  73.8 0.8 fusion.9
  74.6 0.8 add_convert_fusion.1
  75.5 2.6 fusion
  78.1 5.2 %fusion.2 = bf16[2,2,512,512]{3,2,0,1:T(8,128)(2,1)S(1)} fusion(bf16[2,2,512,512]{3,2,0,1:T(8,128)(2,1)} %fusion, bf16[2,1,512,512]{3,2,0,1:T(8,128)(2,1)} %copy-done.9, bf16[2,1,512,512]{3,2,0,1:T(8,128)(2,1)} %copy-done.10, bf16[2,512,512]{2,1,0:T(8,128)(2,1)S(1)} %add_convert_fusion.1), kind=kOutput, calls=%fused_computation.5 | convolution fusion | flops 2157969408 | bytes 7340032 | tf_op jit(solution)/shard_map/rij,rsjk->rsik/dot_general | solution.py:26
  83.3 1.5 slice_bitcast_fusion
  84.8 67.2 %collective-permute-start.14 = (bf16[2,512,512]{2,1,0:T(8,128)(2,1)}, bf16[2,512,512]{2,1,0:T(8,128)(2,1)}, u32[]{:S(2)}, u32[]{:S(2)}) collective-permute-start(bf16[2,512,512]{2,1,0:T(8,128)(2,1)} %get-tuple-element.6), channel_id=1, source_target_pairs={{16,0},{24,8},{32,16},{40,24},{48,32},{56,40},{64,48},{72,56},{80,... | collective-permute-start | bytes 3145736 | tf_op jit(solution)/shard_map/ppermute | solution.py:18
  152.0 1.7 fusion.3
  153.7 4.7 %fusion.5 = bf16[2,512,512]{2,1,0:T(8,128)(2,1)} fusion(bf16[2,512,512]{2,1,0:T(8,128)(2,1)} %subtract_convert_fusion.1, bf16[2,512,512]{2,1,0:T(8,128)(2,1)} %copy-done.5, bf16[2,512,512]{2,1,0:T(8,128)(2,1)} %fusion.3), kind=kOutput, calls=%fused_computation.14 | convolution fusion | flops 1076887552 | bytes 4194304 | tf_op jit(solution)/shard_map/rij,rjk->rik/dot_general | solution.py:22
  158.4 4.4 %collective-permute-start.10 = (bf16[2,512,512]{2,1,0:T(8,128)(2,1)}, bf16[2,512,512]{2,1,0:T(8,128)(2,1)}, u32[]{:S(2)}, u32[]{:S(2)}) collective-permute-start(bf16[2,512,512]{2,1,0:T(8,128)(2,1)} %fusion.5), channel_id=1, source_target_pairs={{16,0},{24,8},{32,16},{40,24},{48,32},{56,40},{64,48},{72,56},{80,... | collective-permute-start | bytes 3145736 | tf_op jit(solution)/shard_map/ppermute | solution.py:18
  162.9 69.1 %collective-permute-done.14 = bf16[2,512,512]{2,1,0:T(8,128)(2,1)} collective-permute-done((bf16[2,512,512]{2,1,0:T(8,128)(2,1)}, bf16[2,512,512]{2,1,0:T(8,128)(2,1)}, u32[]{:S(2)}, u32[]{:S(2)}) %collective-permute-start.14) | collective-permute-done | bytes 1048608 | tf_op jit(solution)/shard_map/ppermute | solution.py:18
  232.0 1.3 fusion.47
  233.3 1.3 collective-permute-start.15
  234.7 1.3 collective-permute-start.13
  236.0 29.7 %collective-permute-done.10 = bf16[2,512,512]{2,1,0:T(8,128)(2,1)} collective-permute-done((bf16[2,512,512]{2,1,0:T(8,128)(2,1)}, bf16[2,512,512]{2,1,0:T(8,128)(2,1)}, u32[]{:S(2)}, u32[]{:S(2)}) %collective-permute-start.10) | collective-permute-done | bytes 1048608 | tf_op jit(solution)/shard_map/ppermute | solution.py:18
  265.7 1.3 fusion.49
  267.0 1.3 collective-permute-start.11
  268.3 1.3 fusion.48
  269.6 1.3 collective-permute-start.9
  270.9 2.0 fusion.24
  272.9 7.1 %collective-permute-done.11 = bf16[1,512,512]{2,1,0:T(8,128)(2,1)S(1)} collective-permute-done((bf16[1,512,512]{2,1,0:T(8,128)(2,1)S(1)}, bf16[1,512,512]{2,1,0:T(8,128)(2,1)S(1)}, u32[]{:S(2)}, u32[]{:S(2)}) %collective-permute-start.11) | collective-permute-done | bytes 524320 | tf_op jit(solution)/shard_map/ppermute | solution.py:12
  280.0 2.1 fusion.19
  282.1 0.7 add_convert_fusion
  282.8 2.6 collective-permute-done.9
  285.4 3.0 %subtract_convert_fusion = bf16[2,512,512]{2,1,0:T(8,128)(2,1)} fusion(f32[2,512,512]{2,1,0:T(8,128)S(1)} %fusion.19, bf16[2,512,512]{2,1,0:T(8,128)(2,1)S(1)} %copy-done.7, bf16[2,512,512]{2,1,0:T(8,128)(2,1)} %collective-permute-done.8, bf16[1,512,512]{2,1,0:T(8,128)(2,1)S(1)} %get-tuple-element.16, bf16[1,512,512]{2,1,0:T(8,128)(2,1)S(1)} %collective-permute-done.9, ...), kind=kOutput, calls=%fused_computation.23 | convolution fusion | flops 540016640 | bytes 7340033 | tf_op jit(solution)/shard_map/rij,rjk->rik/dot_general | solution.py:22
  288.4 3.4 %fusion.7 = bf16[2,512,512]{2,1,0:T(8,128)(2,1)S(1)} fusion(bf16[2,512,512]{2,1,0:T(8,128)(2,1)} %subtract_convert_fusion, bf16[2,512,512]{2,1,0:T(8,128)(2,1)S(1)} %add_convert_fusion), kind=kOutput, calls=%fused_computation.16 | convolution fusion | flops 1076887552 | bytes 3145728 | tf_op jit(solution)/shard_map/rij,rjk->rik/dot_general | solution.py:22
  291.8 2.0 fusion.8
  (37 shorter events, 0.7 us)
Async XLA Ops:
  0.0 1.5 copy-start
  3.2 45.1 %collective-permute-start.6 = (bf16[2,2,512,512]{3,2,0,1:T(8,128)(2,1)}, bf16[2,2,512,512]{3,2,0,1:T(8,128)(2,1)}, u32[]{:S(2)}, u32[]{:S(2)}) collective-permute-start(bf16[2,2,512,512]{3,2,0,1:T(8,128)(2,1)} %pad_maximum_fusion), channel_id=1, source_target_pairs={{8,0},{16,8},{24,16},{32,24},{40,32},{48,40},{56,48},{64,56},{72,6... | collective-permute-start | bytes 6291464 | tf_op jit(solution)/shard_map/ppermute | solution.py:18
  5.4 35.1 %collective-permute-start.2 = (bf16[2,512,512]{2,1,0:T(8,128)(2,1)}, bf16[2,512,512]{2,1,0:T(8,128)(2,1)}, u32[]{:S(2)}, u32[]{:S(2)}) collective-permute-start(bf16[2,512,512]{2,1,0:T(8,128)(2,1)} %bitcast), channel_id=1, source_target_pairs={{8,0},{16,8},{24,16},{32,24},{40,32},{48,40},{56,48},{64,56},{72,6... | collective-permute-start | bytes 3145736 | tf_op jit(solution)/shard_map/ppermute | solution.py:18
  6.0 50.6 %collective-permute-start.4 = (bf16[2,2,512,512]{3,2,0,1:T(8,128)(2,1)}, bf16[2,2,512,512]{3,2,0,1:T(8,128)(2,1)S(1)}, u32[]{:S(2)}, u32[]{:S(2)}) collective-permute-start(bf16[2,2,512,512]{3,2,0,1:T(8,128)(2,1)} %pad_maximum_fusion), channel_id=1, source_target_pairs={{248,0},{0,8},{8,16},{16,24},{24,32},{32,40},{40,48},{48,56},{56,6... | collective-permute-start | bytes 6291464 | tf_op jit(solution)/shard_map/ppermute | solution.py:18
  6.0 39.5 %collective-permute-start = (bf16[2,512,512]{2,1,0:T(8,128)(2,1)}, bf16[2,512,512]{2,1,0:T(8,128)(2,1)}, u32[]{:S(2)}, u32[]{:S(2)}) collective-permute-start(bf16[2,512,512]{2,1,0:T(8,128)(2,1)} %bitcast), channel_id=1, source_target_pairs={{248,0},{0,8},{8,16},{16,24},{24,32},{32,40},{40,48},{48,56},{56,6... | collective-permute-start | bytes 3145736 | tf_op jit(solution)/shard_map/ppermute | solution.py:18
  41.8 12.9 %collective-permute-start.3 = (bf16[1,512,512]{2,1,0:T(8,128)(2,1)S(1)}, bf16[1,512,512]{2,1,0:T(8,128)(2,1)S(1)}, u32[]{:S(2)}, u32[]{:S(2)}) collective-permute-start(bf16[1,512,512]{2,1,0:T(8,128)(2,1)S(1)} %get-tuple-element.22), channel_id=1, source_target_pairs={{1,0},{2,1},{3,2},{4,3},{5,4},{6,5},{7,6},{9,8},{10,9},{11,10},{12... | collective-permute-start | bytes 1572872 | tf_op jit(solution)/shard_map/ppermute | solution.py:12
  46.8 7.8 %copy-start.2 = (bf16[2,1,512,512]{3,2,1,0:T(8,128)(2,1)S(1)}, bf16[2,1,512,512]{3,2,1,0:T(8,128)(2,1)}, u32[]{:S(2)}) copy-start(bf16[2,1,512,512]{3,2,1,0:T(8,128)(2,1)} %param.4) | copy-start | bytes 3145732
  46.8 11.3 %collective-permute-start.1 = (bf16[1,512,512]{2,1,0:T(8,128)(2,1)S(1)}, bf16[1,512,512]{2,1,0:T(8,128)(2,1)S(1)}, u32[]{:S(2)}, u32[]{:S(2)}) collective-permute-start(bf16[1,512,512]{2,1,0:T(8,128)(2,1)S(1)} %get-tuple-element.19), channel_id=1, source_target_pairs={{0,1},{1,2},{2,3},{3,4},{4,5},{5,6},{6,7},{8,9},{9,10},{10,11},{11... | collective-permute-start | bytes 1572872 | tf_op jit(solution)/shard_map/ppermute | solution.py:12
  50.0 16.9 %collective-permute-start.7 = (bf16[1,2,512,512]{3,2,0,1:T(8,128)(2,1)S(1)}, bf16[1,2,512,512]{3,2,0,1:T(8,128)(2,1)S(1)}, u32[]{:S(2)}, u32[]{:S(2)}) collective-permute-start(bf16[1,2,512,512]{3,2,0,1:T(8,128)(2,1)S(1)} %get-tuple-element.10), channel_id=1, source_target_pairs={{1,0},{2,1},{3,2},{4,3},{5,4},{6,5},{7,6},{9,8},{10,9},{11,10},{12... | collective-permute-start | bytes 3145736 | tf_op jit(solution)/shard_map/ppermute | solution.py:12
  56.8 16.7 %collective-permute-start.5 = (bf16[1,2,512,512]{3,2,0,1:T(8,128)(2,1)S(1)}, bf16[1,2,512,512]{3,2,0,1:T(8,128)(2,1)S(1)}, u32[]{:S(2)}, u32[]{:S(2)}) collective-permute-start(bf16[1,2,512,512]{3,2,0,1:T(8,128)(2,1)S(1)} %get-tuple-element.7), channel_id=1, source_target_pairs={{0,1},{1,2},{2,3},{3,4},{4,5},{5,6},{6,7},{8,9},{9,10},{10,11},{11... | collective-permute-start | bytes 3145736 | tf_op jit(solution)/shard_map/ppermute | solution.py:12
  69.5 5.8 %copy-start.9 = (bf16[2,1,512,512]{3,2,0,1:T(8,128)(2,1)}, bf16[2,1,512,512]{3,2,0,1:T(8,128)(2,1)S(1)}, u32[]{:S(2)}) copy-start(bf16[2,1,512,512]{3,2,0,1:T(8,128)(2,1)S(1)} %fusion.10) | copy-start | bytes 3145732
  74.6 1.0 copy-start.10
  75.5 2.6 copy-start.5
  83.3 68.7 %copy-start.6 = (bf16[2,512,512]{2,1,0:T(8,128)(2,1)S(1)}, bf16[2,512,512]{2,1,0:T(8,128)(2,1)}, u32[]{:S(2)}) copy-start(bf16[2,512,512]{2,1,0:T(8,128)(2,1)} %copy-done.5) | copy-start | bytes 3145732
  83.3 68.7 %copy-start.8 = (bf16[2,512,512]{2,1,0:T(8,128)(2,1)S(1)}, bf16[2,512,512]{2,1,0:T(8,128)(2,1)}, u32[]{:S(2)}) copy-start(bf16[2,512,512]{2,1,0:T(8,128)(2,1)} %subtract_convert_fusion.1) | copy-start | bytes 3145732
  84.8 147.2 %collective-permute-start.14 = (bf16[2,512,512]{2,1,0:T(8,128)(2,1)}, bf16[2,512,512]{2,1,0:T(8,128)(2,1)}, u32[]{:S(2)}, u32[]{:S(2)}) collective-permute-start(bf16[2,512,512]{2,1,0:T(8,128)(2,1)} %get-tuple-element.6), channel_id=1, source_target_pairs={{16,0},{24,8},{32,16},{40,24},{48,32},{56,40},{64,48},{72,56},{80,... | collective-permute-start | bytes 3145736 | tf_op jit(solution)/shard_map/ppermute | solution.py:18
  152.0 82.6 %collective-permute-start.12 = (bf16[2,512,512]{2,1,0:T(8,128)(2,1)}, bf16[2,512,512]{2,1,0:T(8,128)(2,1)S(1)}, u32[]{:S(2)}, u32[]{:S(2)}) collective-permute-start(bf16[2,512,512]{2,1,0:T(8,128)(2,1)} %get-tuple-element.5), channel_id=1, source_target_pairs={{240,0},{248,8},{0,16},{8,24},{16,32},{24,40},{32,48},{40,56},{48,... | collective-permute-start | bytes 3145736 | tf_op jit(solution)/shard_map/ppermute | solution.py:18
  158.4 107.3 %collective-permute-start.10 = (bf16[2,512,512]{2,1,0:T(8,128)(2,1)}, bf16[2,512,512]{2,1,0:T(8,128)(2,1)}, u32[]{:S(2)}, u32[]{:S(2)}) collective-permute-start(bf16[2,512,512]{2,1,0:T(8,128)(2,1)} %fusion.5), channel_id=1, source_target_pairs={{16,0},{24,8},{32,16},{40,24},{48,32},{56,40},{64,48},{72,56},{80,... | collective-permute-start | bytes 3145736 | tf_op jit(solution)/shard_map/ppermute | solution.py:18
  162.9 105.5 %collective-permute-start.8 = (bf16[2,512,512]{2,1,0:T(8,128)(2,1)}, bf16[2,512,512]{2,1,0:T(8,128)(2,1)}, u32[]{:S(2)}, u32[]{:S(2)}) collective-permute-start(bf16[2,512,512]{2,1,0:T(8,128)(2,1)} %fusion.5), channel_id=1, source_target_pairs={{240,0},{248,8},{0,16},{8,24},{16,32},{24,40},{32,48},{40,56},{48,... | collective-permute-start | bytes 3145736 | tf_op jit(solution)/shard_map/ppermute | solution.py:18
  233.3 37.6 %collective-permute-start.15 = (bf16[1,512,512]{2,1,0:T(8,128)(2,1)S(1)}, bf16[1,512,512]{2,1,0:T(8,128)(2,1)S(1)}, u32[]{:S(2)}, u32[]{:S(2)}) collective-permute-start(bf16[1,512,512]{2,1,0:T(8,128)(2,1)S(1)} %get-tuple-element.14), channel_id=1, source_target_pairs={{1,0},{2,1},{3,2},{4,3},{5,4},{6,5},{7,6},{9,8},{10,9},{11,10},{12... | collective-permute-start | bytes 1572872 | tf_op jit(solution)/shard_map/ppermute | solution.py:12
  234.6 32.4 %copy-start.3 = (bf16[2,512,512]{2,1,0:T(8,128)(2,1)}, bf16[2,512,512]{2,1,0:T(8,128)(2,1)S(1)}, u32[]{:S(2)}) copy-start(bf16[2,512,512]{2,1,0:T(8,128)(2,1)S(1)} %collective-permute-done.12) | copy-start | bytes 3145732
  234.7 47.4 %collective-permute-start.13 = (bf16[1,512,512]{2,1,0:T(8,128)(2,1)S(1)}, bf16[1,512,512]{2,1,0:T(8,128)(2,1)S(1)}, u32[]{:S(2)}, u32[]{:S(2)}) collective-permute-start(bf16[1,512,512]{2,1,0:T(8,128)(2,1)S(1)} %get-tuple-element.11), channel_id=1, source_target_pairs={{0,1},{1,2},{2,3},{3,4},{4,5},{5,6},{6,7},{8,9},{9,10},{10,11},{11... | collective-permute-start | bytes 1572872 | tf_op jit(solution)/shard_map/ppermute | solution.py:12
  267.0 13.0 %collective-permute-start.11 = (bf16[1,512,512]{2,1,0:T(8,128)(2,1)S(1)}, bf16[1,512,512]{2,1,0:T(8,128)(2,1)S(1)}, u32[]{:S(2)}, u32[]{:S(2)}) collective-permute-start(bf16[1,512,512]{2,1,0:T(8,128)(2,1)S(1)} %get-tuple-element.18), channel_id=1, source_target_pairs={{1,0},{2,1},{3,2},{4,3},{5,4},{6,5},{7,6},{9,8},{10,9},{11,10},{12... | collective-permute-start | bytes 1572872 | tf_op jit(solution)/shard_map/ppermute | solution.py:12
  269.6 15.8 %collective-permute-start.9 = (bf16[1,512,512]{2,1,0:T(8,128)(2,1)S(1)}, bf16[1,512,512]{2,1,0:T(8,128)(2,1)S(1)}, u32[]{:S(2)}, u32[]{:S(2)}) collective-permute-start(bf16[1,512,512]{2,1,0:T(8,128)(2,1)S(1)} %get-tuple-element.15), channel_id=1, source_target_pairs={{0,1},{1,2},{2,3},{3,4},{4,5},{5,6},{6,7},{8,9},{9,10},{10,11},{11... | collective-permute-start | bytes 1572872 | tf_op jit(solution)/shard_map/ppermute | solution.py:12
  280.0 2.1 copy-start.4
  282.1 3.3 %copy-start.7 = (bf16[2,512,512]{2,1,0:T(8,128)(2,1)S(1)}, bf16[2,512,512]{2,1,0:T(8,128)(2,1)}, u32[]{:S(2)}) copy-start(bf16[2,512,512]{2,1,0:T(8,128)(2,1)} %fusion.5) | copy-start | bytes 3145732
  288.4 3.4 %copy-start.1 = (bf16[2,512,512]{2,1,0:T(8,128)(2,1)S(1)}, bf16[2,512,512]{2,1,0:T(8,128)(2,1)}, u32[]{:S(2)}) copy-start(bf16[2,512,512]{2,1,0:T(8,128)(2,1)} %subtract_convert_fusion) | copy-start | bytes 3145732
where the time goes:
time: 295 us; the launch traced here: 294 us
  waiting for transfers between devices  152 us (52%)
  starting transfers between devices  90.7 us (31%)
  matrix products  35.7 us (12%)
  local copies, waits for them, and re-layouts  10.1 us (3%)
  other arithmetic  5.24 us (2%)
    ppermute x8, waiting for transfers between devices, from_behind_2(): return lax.ppermute(block, axis, route)  133 us
    ppermute x8, starting transfers between devices, from_behind_2(): return lax.ppermute(block, axis, route)  75.4 us
    dot_general x14, matrix products, batch_product(): jnp.einsum('rij,rjk->rik', left, right, preferred_element_type=jnp.float32)  27.9 us
    ppermute x8, waiting for transfers between devices, from_behind(): lax.ppermute(value, axis, [(source, source + steps) for source in range(l...  18.3 us
    ppermute x8, starting transfers between devices, from_behind(): lax.ppermute(value, axis, [(source, source + steps) for source in range(l...  15.3 us
    dot_general x2, matrix products, pair_product(): jnp.einsum('rij,rsjk->rsik', left, right, preferred_element_type=jnp.floa...  7.78 us
  transfers between devices with their start and end apart: 16, of which 8 were waited for; matrix products, arithmetic and copies ran while one was open for 10% of the time, Pallas kernels for 0%

commit v1 on v0

v1 whole, which is shorter than its diff:
```python
import jax
import jax.numpy as jnp
from jax import lax
from jax.experimental import pallas as pl
from jax.experimental.pallas import tpu as pltpu
from jax.sharding import PartitionSpec as P

MESH = pl.DeviceIdType.MESH
W = 512
PIECES = 4
PIECE = W // PIECES
L, U, F = 0, 1, 2
FIRST_COLUMNS = ((0, 256), (256, 256))
LAST_COLUMNS = ((0, 256), (256, 128), (384, 128))


def dot(left, right):
    return jnp.dot(left, right, preferred_element_type=jnp.float32)


def device_at(x, y, z, core):
    return (z * 4 + y // 2 * 2 + core, y % 2 * 4 + x)


def chip_of_row(row):
    return row % 8 // 2, row % 2 * 2 + 1 - row // 8


def piece(ref, kind, index):
    span = pl.ds(index * PIECE, PIECE)
    return ref.at[:, span] if kind == F else ref.at[span]


def kernel(
    lower, upper, rhs, out,
    own, near, corr, terms, inner, one, far, result,
    in_send, in_recv, core_send, halo_send, near_recv,
    far_send, far_recv, out_send, out_recv,
):
    cuts, col = lax.axis_index("cuts"), lax.axis_index("col")
    x, z, core = col % 4, cuts // 4, cuts % 2
    half = cuts // 2 % 2
    y = half * 2 + col // 4
    parity = 1 - y % 2
    row = parity * 8 + x * 2 + half
    next_x, next_y = chip_of_row((row + 1) % 16)
    prev_x, prev_y = chip_of_row((row + 15) % 16)
    end, start = z == 7, z == 0
    next_x, next_y = jnp.where(end, next_x, x), jnp.where(end, next_y, y)
    prev_x, prev_y = jnp.where(start, prev_x, x), jnp.where(start, prev_y, y)
    next_z, prev_z = (z + 1) % 8, (z + 7) % 8

    sides = [device_at(x, 2 * side + parity, z, core) for side in (0, 1)]
    twin = device_at(x, y, z, 1 - core)
    following = device_at(next_x, next_y, next_z, core)
    preceding = device_at(prev_x, prev_y, prev_z, core)
    upward = core == 1
    halo = device_at(
        jnp.where(upward, next_x, prev_x),
        jnp.where(upward, next_y, prev_y),
        jnp.where(upward, next_z, prev_z),
        1 - core,
    )

    barrier = pltpu.get_barrier_semaphore()
    for partner in (*sides, twin, following, preceding, halo):
        pl.semaphore_signal(barrier, inc=1, device_id=partner, device_id_type=MESH)
    pl.semaphore_wait(barrier, 6)

    sent = []

    def send(source, target, send_sem, recv_sem, device):
        copy = pltpu.make_async_remote_copy(
            src_ref=source,
            dst_ref=target,
            send_sem=send_sem,
            recv_sem=recv_sem,
            device_id=device,
            device_id_type=MESH,
        )
        copy.start()
        sent.append(copy)

    def arrive(target, recv_sem):
        pltpu.make_async_remote_copy(
            src_ref=target,
            dst_ref=target,
            send_sem=recv_sem,
            recv_sem=recv_sem,
            device_id=twin,
            device_id_type=MESH,
        ).wait_recv()

    for kind, source in ((L, lower), (U, upper), (F, rhs)):
        for index in range(PIECES):
            for side in (0, 1):
                send(
                    piece(source.at[side], kind, index),
                    piece(own.at[half, kind], kind, index),
                    in_send.at[side, kind, index],
                    in_recv.at[half, kind, index],
                    sides[side],
                )

    first_slice = (row == 0) & start & (core == 0)
    last_slice = (row == 15) & end & (core == 1)

    def forward(kind, index):
        for slot in (0, 1):
            part = piece(own.at[slot, kind], kind, index)
            arrive(part, in_recv.at[slot, kind, index])
            edge = {(0, L): first_slice, (1, U): last_slice}.get((slot, kind))
            if edge is not None:

                @pl.when(edge)
                def _(part=part):
                    part[...] = jnp.zeros(part.shape, part.dtype)

            send(
                part,
                piece(near.at[slot + core, kind], kind, index),
                core_send.at[slot, kind, index],
                near_recv.at[slot + core, kind, index],
                twin,
            )
        send(
            piece(own.at[core, kind], kind, index),
            piece(near.at[2 - 2 * core, kind], kind, index),
            halo_send.at[kind, index],
            near_recv.at[2 - 2 * core, kind, index],
            halo,
        )

    def settle(kind, index):
        for slot in range(3):
            arrive(piece(near.at[slot, kind], kind, index), near_recv.at[slot, kind, index])

    def horner(matrix, values, columns, store):
        span = pl.ds(*columns)
        wide = lambda: values[:, span].astype(jnp.float32)
        inner[0, :, span] = (wide() + dot(matrix[...], values[:, span])).astype(jnp.bfloat16)
        inner[1, :, span] = (wide() + dot(matrix[...], inner[0, :, span])).astype(jnp.bfloat16)
        store[:, span] = (wide() + dot(matrix[...], inner[1, :, span])).astype(jnp.bfloat16)

    whole = (0, W)

    def correct(slot):
        corr[slot] = (
            dot(own[slot, L], near[slot, U]) + dot(own[slot, U], near[slot + 1, L])
        ).astype(jnp.bfloat16)

    def couple(slot, kind):
        other = near.at[slot + kind, kind]
        terms[slot, kind] = (-dot(own[slot, kind], other[...])).astype(jnp.bfloat16)

    def reduce_block(slot, kind):
        horner(corr.at[slot], terms.at[slot, kind], whole, one.at[slot, kind])

    def reduce_right(columns):
        span = pl.ds(*columns)
        for slot in (0, 1):
            terms[slot, F, :, span] = (
                own[slot, F, :, span].astype(jnp.float32)
                - dot(own[slot, L], near[slot, F, :, span])
                - dot(own[slot, U], near[slot + 1, F, :, span])
            ).astype(jnp.bfloat16)
            horner(corr.at[slot], terms.at[slot, F], columns, one.at[slot, F])

    def send_block(slot, kind, device):
        send(
            one.at[slot, kind],
            far.at[1 - slot, 0],
            far_send.at[1 - slot, PIECES],
            far_recv.at[1 - slot, PIECES],
            device,
        )

    def send_right(index):
        for slot, device in ((0, preceding), (1, following)):
            send(
                piece(one.at[slot, F], F, index),
                piece(far.at[1 - slot, 1], F, index),
                far_send.at[1 - slot, index],
                far_recv.at[1 - slot, index],
                device,
            )

    for index in range(PIECES):
        forward(L, index)
    for index in range(PIECES):
        settle(L, index)
    couple(0, L)
    couple(1, L)
    for index in range(PIECES):
        forward(U, index)
    for index in range(PIECES):
        settle(U, index)
    correct(0)
    reduce_block(0, L)
    send_block(0, L, preceding)
    correct(1)
    couple(1, U)
    reduce_block(1, U)
    send_block(1, U, following)
    forward(F, 0)
    couple(0, U)
    reduce_block(0, U)
    reduce_block(1, L)
    forward(F, 1)
    forward(F, 2)
    settle(F, 0)
    settle(F, 1)
    reduce_right(FIRST_COLUMNS[0])
    send_right(0)
    send_right(1)
    forward(F, 3)
    settle(F, 2)
    settle(F, 3)
    reduce_right(FIRST_COLUMNS[1])
    send_right(2)
    send_right(3)

    for side in (0, 1):
        arrive(far.at[side, 0], far_recv.at[side, PIECES])
    corr[0] = (dot(one[0, L], far[0, 0]) + dot(one[0, U], one[1, L])).astype(jnp.bfloat16)
    corr[1] = (dot(one[1, L], one[0, U]) + dot(one[1, U], far[1, 0])).astype(jnp.bfloat16)
    for columns in LAST_COLUMNS:
        span = pl.ds(*columns)
        indices = range(columns[0] // PIECE, (columns[0] + columns[1]) // PIECE)
        for index in indices:
            for side in (0, 1):
                arrive(piece(far.at[side, 1], F, index), far_recv.at[side, index])
        below = (far.at[0, 1], one.at[0, F])
        above = (one.at[1, F], far.at[1, 1])
        for slot in (0, 1):
            terms[slot, F, :, span] = (
                one[slot, F, :, span].astype(jnp.float32)
                - dot(one[slot, L], below[slot][:, span])
                - dot(one[slot, U], above[slot][:, span])
            ).astype(jnp.bfloat16)
            horner(corr.at[slot], terms.at[slot, F], columns, result.at[slot])
            for index in indices:
                send(
                    piece(result.at[slot], F, index),
                    piece(out.at[half], F, index),
                    out_send.at[slot, index],
                    out_recv.at[half, index],
                    sides[slot],
                )
    for index in range(PIECES):
        for side in (0, 1):
            arrive(piece(out.at[side], F, index), out_recv.at[side, index])
    for copy in sent:
        copy.wait_send()


def on_device(lower, upper, rhs):
    blocks = lambda *lead: pltpu.VMEM((*lead, W, W), jnp.bfloat16)
    copies = lambda *lead: pltpu.SemaphoreType.DMA(lead)
    hbm = pl.BlockSpec(memory_space=pl.ANY)
    reduced = pl.pallas_call(
        kernel,
        out_shape=jax.ShapeDtypeStruct((2, W, W), jnp.bfloat16),
        in_specs=[hbm] * 3,
        out_specs=hbm,
        scratch_shapes=[
            blocks(2, 3),
            blocks(3, 3),
            blocks(2),
            blocks(2, 3),
            blocks(2),
            blocks(2, 3),
            blocks(2, 2),
            blocks(2),
            copies(2, 3, PIECES),
            copies(2, 3, PIECES),
            copies(2, 3, PIECES),
            copies(3, PIECES),
            copies(3, 3, PIECES),
            copies(2, PIECES + 1),
            copies(2, PIECES + 1),
            copies(2, PIECES),
            copies(2, PIECES),
        ],
        compiler_params=pltpu.CompilerParams(
            collective_id=0, has_side_effects=True, vmem_limit_bytes=48 * 2**20
        ),
    )(lower[:, 0], upper[:, 0], rhs[:, 0])
    return reduced.astype(jnp.float32)[:, None]


def solution(mesh):
    return jax.shard_map(
        on_device,
        mesh=mesh,
        in_specs=(P("col", "cuts", None, None),) * 3,
        out_specs=P("col", "cuts", None, None),
        check_vma=False,
    )
```

time: 295 us -> 111 us (0.38)
  the two profiles are of different devices: /device:TPU:174 before, /device:TPU:7 now
where the time goes in v1:
time: 111 us; the launch traced here: 110 us
  Pallas kernels  105 us (95%)
  local copies, waits for them, and re-layouts  3.67 us (3%)
  other arithmetic  1.61 us (1%)
    pallas_call x1, Pallas kernels, on_device(): pl.pallas_call(kernel, out_shape=jax.ShapeDtypeStruct((2, W, W), jnp.bflo...  105 us
    unnamed x6, local copies, waits for them, and re-layouts  3.67 us

profile of v1, /device:TPU:7, one launch (start us, length us, event | category | flops | bytes accessed | tf_op | source)
XLA Modules:
  0.0 110.3 jit_solution(16577939220943582539)
XLA Ops:
  0.0 0.0 copy-start
  0.0 1.2 %copy-done = bf16[2,1,512,512]{3,2,1,0:T(8,128)(2,1)S(1)} copy-done((bf16[2,1,512,512]{3,2,1,0:T(8,128)(2,1)S(1)}, bf16[2,1,512,512]{3,2,1,0:T(8,128)(2,1)}, u32[]{:S(2)}) %copy-start) | copy-done | bytes 1048600
  1.2 0.0 copy-start.1
  1.2 1.2 %copy-done.1 = bf16[2,1,512,512]{3,2,1,0:T(8,128)(2,1)S(1)} copy-done((bf16[2,1,512,512]{3,2,1,0:T(8,128)(2,1)S(1)}, bf16[2,1,512,512]{3,2,1,0:T(8,128)(2,1)}, u32[]{:S(2)}) %copy-start.1) | copy-done | bytes 1048600
  2.5 0.0 copy-start.2
  2.5 1.2 %copy-done.2 = bf16[2,1,512,512]{3,2,1,0:T(8,128)(2,1)S(1)} copy-done((bf16[2,1,512,512]{3,2,1,0:T(8,128)(2,1)S(1)}, bf16[2,1,512,512]{3,2,1,0:T(8,128)(2,1)}, u32[]{:S(2)}) %copy-start.2) | copy-done | bytes 1048600
  3.7 105.0 %shard_map.37 = bf16[2,512,512]{2,1,0:T(8,128)(2,1)S(1)} custom-call(bf16[2,512,512]{2,1,0:T(8,128)(2,1)S(1)} %bitcast.9, bf16[2,512,512]{2,1,0:T(8,128)(2,1)S(1)} %bitcast.10, bf16[2,512,512]{2,1,0:T(8,128)(2,1)S(1)} %bitcast.11), custom_call_target="tpu_custom_call" | custom-call | tf_op jit(solution)/shard_map/pallas_call | solution.py:261
  108.7 1.6 %bitcast_convert_fusion = f32[2,1,512,512]{3,2,1,0:T(8,128)} fusion(bf16[2,512,512]{2,1,0:T(8,128)(2,1)S(1)} %shard_map.37), kind=kLoop, calls=%fused_computation | loop fusion | flops 524288 | bytes 3145728 | tf_op jit(solution)/shard_map/broadcast_in_dim | solution.py:289
Async XLA Ops:
  0.0 1.2 %copy-start = (bf16[2,1,512,512]{3,2,1,0:T(8,128)(2,1)S(1)}, bf16[2,1,512,512]{3,2,1,0:T(8,128)(2,1)}, u32[]{:S(2)}) copy-start(bf16[2,1,512,512]{3,2,1,0:T(8,128)(2,1)} %param.3) | copy-start | bytes 3145732
  1.2 1.2 %copy-start.1 = (bf16[2,1,512,512]{3,2,1,0:T(8,128)(2,1)S(1)}, bf16[2,1,512,512]{3,2,1,0:T(8,128)(2,1)}, u32[]{:S(2)}) copy-start(bf16[2,1,512,512]{3,2,1,0:T(8,128)(2,1)} %param.4) | copy-start | bytes 3145732
  2.5 1.2 %copy-start.2 = (bf16[2,1,512,512]{3,2,1,0:T(8,128)(2,1)S(1)}, bf16[2,1,512,512]{3,2,1,0:T(8,128)(2,1)}, u32[]{:S(2)}) copy-start(bf16[2,1,512,512]{3,2,1,0:T(8,128)(2,1)} %param.5) | copy-start | bytes 3145732

commit v2 on v0

v2 whole, which is shorter than its diff:
```python
import jax
import jax.numpy as jnp
from jax import lax
from jax.experimental import pallas as pl
from jax.experimental.pallas import tpu as pltpu
from jax.sharding import PartitionSpec as P

MESH = pl.DeviceIdType.MESH
W = 512
PIECES = 4
PIECE = W // PIECES
RELAYED = (3,)
L, U, F = 0, 1, 2
COLUMNS = ((0, 256), (256, 256))


def dot(left, right):
    return jnp.dot(left, right, preferred_element_type=jnp.float32)


def device_at(x, y, z, core):
    return (z * 4 + y // 2 * 2 + core, y % 2 * 4 + x)


def chip_of_row(row):
    return row % 8 // 2, row % 2 * 2 + row // 8


def piece(ref, kind, index):
    span = pl.ds(index * PIECE, PIECE)
    return ref.at[:, span] if kind == F else ref.at[span]


def choose(condition, first, second):
    return tuple(jnp.where(condition, one, other) for one, other in zip(first, second))


def flip(chip):
    return chip[0], (chip[1] + 2) % 4


def kernel(
    lower, upper, rhs, out,
    mine, near, relay, corr, left_terms, right_terms, sources, left_one, right_one, fields, inner, result,
    keep_sem, in_send, relay_send, relay_recv, extra_send, mine_recv, near_recv,
    twin_send, chain_send, cross_send, halo_send, out_send, out_recv,
):
    cuts, col = lax.axis_index("cuts"), lax.axis_index("col")
    x, low, z, core = col % 4, col // 4, cuts // 4, cuts % 2
    half = cuts // 2 % 2
    y = half * 2 + low
    row = low * 8 + x * 2 + half
    top, bottom = z == 7, z == 0
    first, second = half == 0, half == 1
    lead = (top & second) | (bottom & first)
    trail = (top & first) | (bottom & second)

    next_z, prev_z = (z + 1) % 8, (z + 7) % 8
    next_chip = choose(top, chip_of_row((row + 1) % 16), (x, y))
    prev_chip = choose(bottom, chip_of_row((row + 15) % 16), (x, y))
    has_next, has_prev = ~(top & (row == 15)), ~(bottom & (row == 0))
    partner = device_at(x, (y + 2) % 4, z, core)
    twin = device_at(x, y, z, 1 - core)
    following, following_cross = (device_at(*next_chip, next_z, c) for c in (core, 1 - core))
    preceding, preceding_cross = (device_at(*prev_chip, prev_z, c) for c in (core, 1 - core))

    end = top | bottom
    end_z = jnp.where(top, 0, 7)
    end_chip = choose(top, next_chip, prev_chip)
    has_end = jnp.where(top, has_next, has_prev) & end
    partner_row = row + 1 - 2 * half
    step = jnp.where(top, 1, 15)
    partner_end = chip_of_row((partner_row + step) % 16)
    partner_has_end = end & ~(top & (partner_row == 15)) & ~(bottom & (partner_row == 0))
    goal, goal_cross = (device_at(*partner_end, end_z, c) for c in (core, 1 - core))
    origin, origin_cross = (device_at(*flip(end_chip), end_z, c) for c in (core, 1 - core))
    chain_end, chain_end_cross = (device_at(*end_chip, end_z, c) for c in (core, 1 - core))
    crosses = (top & (core == 1)) | (bottom & (core == 0))

    def copy_in(kind, source):
        return pltpu.make_async_copy(source.at[half], mine.at[1 + half, kind], keep_sem.at[kind])

    kinds = ((L, lower), (U, upper), (F, rhs))
    for kind, source in kinds:
        copy_in(kind, source).start()

    barrier = pltpu.get_barrier_semaphore()

    def greet(device, condition):
        @pl.when(condition)
        def _():
            pl.semaphore_signal(barrier, inc=1, device_id=device, device_id_type=MESH)

    greet(partner, core < 2)
    greet(twin, core < 2)
    greet(following, ~top)
    greet(preceding, ~bottom)
    greet(following_cross, ~top & (core == 1))
    greet(preceding_cross, ~bottom & (core == 0))
    greet(chain_end, has_end & lead)
    greet(origin, has_end)
    greet(origin_cross, has_end & lead & crosses)
    greet(chain_end_cross, has_end & trail & crosses)
    expected = (
        ~top,
        ~bottom,
        ~top & (core == 1),
        ~bottom & (core == 0),
        has_end & lead,
        partner_has_end,
        partner_has_end & trail & crosses,
        has_end & trail & crosses,
    )
    pl.semaphore_wait(barrier, 2 + sum(flag.astype(jnp.int32) for flag in expected))

    sent = []

    def only(condition, action):
        if condition is None:
            action()
        else:
            pl.when(condition)(action)

    gate = [None]

    def gated(condition):
        if gate[0] is None:
            return condition
        return gate[0] if condition is None else gate[0] & condition

    def send(source, target, send_sem, recv_sem, device, condition=None):
        condition = gated(condition)
        copy = pltpu.make_async_remote_copy(
            src_ref=source,
            dst_ref=target,
            send_sem=send_sem,
            recv_sem=recv_sem,
            device_id=device,
            device_id_type=MESH,
        )
        only(condition, copy.start)
        sent.append((condition, copy))

    def arrive(target, recv_sem, condition=None):
        condition = gated(condition)
        copy = pltpu.make_async_remote_copy(
            src_ref=target,
            dst_ref=target,
            send_sem=recv_sem,
            recv_sem=recv_sem,
            device_id=twin,
            device_id_type=MESH,
        )
        only(condition, copy.wait_recv)

    def to_mine(source, slot, kind, index, send_sem, device, condition):
        send(
            source,
            piece(mine.at[slot, kind], kind, index),
            send_sem,
            mine_recv.at[slot, kind, index],
            device,
            condition,
        )

    def to_near(source, slot, kind, index, send_sem, device, condition=None):
        send(
            source,
            piece(near.at[slot, kind], kind, index),
            send_sem,
            near_recv.at[slot, kind, index],
            device,
            condition,
        )

    mine_end = jnp.where(top, 0, 3)
    near_end = jnp.where(top, 0, 4)

    def reaches(kind, upward):
        return kind == F or (kind == U) == upward

    for kind, source in kinds:
        for index in range(PIECES):
            other = piece(source.at[1 - half], kind, index)
            to_mine(other, 1 + half, kind, index, in_send.at[kind, index], partner, None)
            to_mine(other, mine_end, kind, index, extra_send.at[0, kind, index], goal, lead)
            if index in RELAYED:
                send(
                    piece(source.at[half], kind, index),
                    piece(relay.at[kind], kind, index),
                    relay_send.at[0, kind, index],
                    relay_recv.at[kind, index],
                    partner,
                    lead & has_end,
                )
            for upward, side in ((True, top), (False, bottom)):
                if reaches(kind, upward):
                    to_near(
                        other,
                        0 if upward else 4,
                        kind,
                        index,
                        extra_send.at[1 if upward else 2, kind, index],
                        goal_cross,
                        trail & partner_has_end & crosses & side,
                    )

    first_slice = (row == 0) & bottom & (core == 0)
    last_slice = (row == 15) & top & (core == 1)

    def blank(ref, condition):
        condition = gated(condition)

        @pl.when(condition)
        def _():
            ref[...] = jnp.zeros(ref.shape, ref.dtype)

    blank(mine.at[0], ~has_prev)
    blank(mine.at[3], ~has_next)
    blank(near.at[0], ~has_prev & (core == 0))
    blank(near.at[4], ~has_next & (core == 1))

    def cut(slot, kind, part):
        if kind != F:
            blank(part, (first_slice & (slot == 1)) if kind == L else (last_slice & (slot == 2)))

    def pass_on(slot, kind, index, local):
        part = piece(mine.at[slot, kind], kind, index)
        number = 0 if local else 1
        to_near(part, slot + core, kind, index, twin_send.at[number, kind, index], twin)
        upward = second if local else first
        if local:
            chain = ~lead if index in RELAYED else None
        else:
            chain = ~trail
        for way, device, there, target in (
            (upward, following, has_next, 0),
            (~upward, preceding, has_prev, 3),
        ):
            condition = way & there if chain is None else way & there & chain
            to_mine(part, target, kind, index, chain_send.at[number, target // 3, kind, index], device, condition)
        cross = (core != half) if local else (core == half) & ~lead
        for way, device, there, target in (
            (core == 1, following_cross, has_next, 0),
            (core == 0, preceding_cross, has_prev, 4),
        ):
            if reaches(kind, target == 0):
                to_near(
                    part,
                    target,
                    kind,
                    index,
                    cross_send.at[number, target // 4, kind, index],
                    device,
                    way & there & cross,
                )

    def local(kind):
        copy_in(kind, kinds[kind][1]).wait()
        cut(1 + half, kind, mine.at[1 + half, kind])
        for index in range(PIECES):
            pass_on(1 + half, kind, index, True)

    def forward(kind, index):
        part = piece(mine.at[2 - half, kind], kind, index)
        arrive(part, mine_recv.at[2 - half, kind, index])
        cut(2 - half, kind, part)
        pass_on(2 - half, kind, index, False)
        if index in RELAYED:
            part = piece(relay.at[kind], kind, index)
            waiting = trail & partner_has_end
            arrive(part, relay_recv.at[kind, index], waiting)
            to_mine(part, mine_end, kind, index, relay_send.at[1, kind, index], goal, waiting)

    def halo(kind, index):
        for slot, there in ((0, has_prev), (3, has_next)):
            part = piece(mine.at[slot, kind], kind, index)
            arrive(part, mine_recv.at[slot, kind, index], there)
            upward = slot == 0
            condition = None if reaches(kind, upward) else (core == 1) if upward else (core == 0)
            to_near(
                part, slot + core, kind, index, halo_send.at[slot // 3, kind, index], twin, condition
            )

    def settle(slot, kind, index):
        if slot in (0, 4) and not reaches(kind, slot == 0):
            return
        condition = {0: (core == 1) | has_prev, 4: (core == 0) | has_next}.get(slot)
        arrive(piece(near.at[slot, kind], kind, index), near_recv.at[slot, kind, index], condition)

    def settle_blocks(*slots):
        for slot in slots:
            for kind in (L, U):
                for index in range(PIECES):
                    settle(slot, kind, index)

    def horner(jobs):
        for step in range(3):
            for number, (matrix, values, store) in enumerate(jobs):
                width = values.shape[1]
                last = values if step == 0 else inner.at[number, step - 1, :, pl.ds(0, width)]
                target = store if step == 2 else inner.at[number, step, :, pl.ds(0, width)]
                target[...] = (values[...].astype(jnp.float32) + dot(matrix[...], last[...])).astype(
                    jnp.bfloat16
                )

    def correct(k):
        corr[k] = (dot(mine[k, L], near[k, U]) + dot(mine[k, U], near[k + 1, L])).astype(jnp.bfloat16)

    def couple_left(k):
        left_terms[k] = (-dot(mine[k, L], near[k, L])).astype(jnp.bfloat16)
        return corr.at[k], left_terms.at[k], left_one.at[k]

    def couple_right(k):
        right_terms[k] = (-dot(mine[k, U], near[k + 1, U])).astype(jnp.bfloat16)
        return corr.at[k], right_terms.at[k], right_one.at[k]

    def source(values, left, right, before, after, span):
        return (
            values[:, span].astype(jnp.float32)
            - dot(left[...], before[:, span])
            - dot(right[...], after[:, span])
        ).astype(jnp.bfloat16)

    def forward_if(condition, index):
        gate[0] = condition
        forward(F, index)
        gate[0] = None

    def settle_if(condition, *slots):
        gate[0] = condition
        settle_blocks(*slots)
        gate[0] = None

    every = range(PIECES)
    inside = ~end
    local(L)
    local(U)
    for kind in (L, U):
        for index in every:
            forward(kind, index)
    local(F)
    for index in every:
        halo(L, index)
    settle_blocks(2)
    settle_if(core == 0, 3)
    settle_if(core == 1, 1)
    k = 2 - core
    correct(k)
    horner([couple_left(k), couple_right(k)])
    forward_if(inside, 0)
    forward_if(inside, 1)
    for index in every:
        halo(U, index)
    forward_if(end, 0)
    settle_if(core == 0, 1)
    settle_if(core == 1, 3)
    k = 1 + core
    correct(k)
    horner([couple_left(k), couple_right(k)])
    forward_if(inside, 2)
    forward_if(end, 1)
    settle_blocks(0, 4)
    correct(0)
    correct(3)
    horner([couple_right(0), couple_left(3)])
    forward_if(inside, 3)
    forward_if(end, 2)

    for k in (1, 2):
        corr[3 + k] = (
            dot(left_one[k], right_one[k - 1]) + dot(right_one[k], left_one[k + 1])
        ).astype(jnp.bfloat16)

    def home_copy(slot, index):
        return pltpu.make_async_copy(
            piece(result.at[slot], F, index), piece(out.at[half], F, index), keep_sem.at[3 + index]
        )

    def send_out(slot, index):
        pl.when(half == slot)(home_copy(slot, index).start)
        send(
            piece(result.at[slot], F, index),
            piece(out.at[half], F, index),
            out_send.at[index],
            out_recv.at[index],
            partner,
            half != slot,
        )

    for columns in COLUMNS:
        span = pl.ds(*columns)
        indices = range(columns[0] // PIECE, (columns[0] + columns[1]) // PIECE)
        for index in indices:
            halo(F, index)
        if columns[0] == 0:
            forward_if(end, 3)
        for index in indices:
            for slot in range(5):
                settle(slot, F, index)
        jobs = []
        for k in range(4):
            sources[k, :, span] = source(
                mine.at[k, F], mine.at[k, L], mine.at[k, U], near.at[k, F], near.at[k + 1, F], span
            )
            jobs.append((corr.at[k], sources.at[k, :, span], fields.at[k, :, span]))
        horner(jobs)
        jobs = []
        for slot in (0, 1):
            k = slot + 1
            sources[k, :, span] = source(
                fields.at[k], left_one.at[k], right_one.at[k], fields.at[k - 1], fields.at[k + 1], span
            )
            jobs.append((corr.at[3 + k], sources.at[k, :, span], result.at[slot, :, span]))
        horner(jobs)
        for slot in (0, 1):
            for index in indices:
                send_out(slot, index)
    for index in range(PIECES):
        for slot in (0, 1):
            pl.when(half == slot)(home_copy(slot, index).wait)
        arrive(piece(out.at[1 - half], F, index), out_recv.at[index])
    for condition, copy in sent:
        only(condition, copy.wait_send)


def on_device(lower, upper, rhs):
    blocks = lambda *lead: pltpu.VMEM((*lead, W, W), jnp.bfloat16)
    copies = lambda *lead: pltpu.SemaphoreType.DMA(lead)
    hbm = pl.BlockSpec(memory_space=pltpu.HBM)
    reduced = pl.pallas_call(
        kernel,
        out_shape=jax.ShapeDtypeStruct((2, W, W), jnp.bfloat16),
        in_specs=[hbm] * 3,
        out_specs=pl.BlockSpec(memory_space=pl.ANY),
        scratch_shapes=[
            blocks(4, 3),
            blocks(5, 3),
            blocks(3),
            blocks(6),
            blocks(4),
            blocks(4),
            blocks(4),
            blocks(4),
            blocks(4),
            blocks(4),
            blocks(4, 2),
            blocks(2),
            copies(3 + PIECES),
            copies(3, PIECES),
            copies(2, 3, PIECES),
            copies(3, PIECES),
            copies(3, 3, PIECES),
            copies(4, 3, PIECES),
            copies(5, 3, PIECES),
            copies(2, 3, PIECES),
            copies(2, 2, 3, PIECES),
            copies(2, 2, 3, PIECES),
            copies(2, 3, PIECES),
            copies(PIECES),
            copies(PIECES),
        ],
        compiler_params=pltpu.CompilerParams(
            collective_id=0, has_side_effects=True, vmem_limit_bytes=60 * 2**20
        ),
    )(lower[:, 0], upper[:, 0], rhs[:, 0])
    return reduced.astype(jnp.float32)[:, None]


def solution(mesh):
    return jax.shard_map(
        on_device,
        mesh=mesh,
        in_specs=(P("col", "cuts", None, None),) * 3,
        out_specs=P("col", "cuts", None, None),
        check_vma=False,
    )
```

time: 295 us -> 101 us (0.34)
  the two profiles are of different devices: /device:TPU:174 before, /device:TPU:1 now
where the time goes in v2:
time: 101 us
  Pallas kernels  98.2 us (97%)
  other arithmetic  2.84 us (3%)
    pallas_call x1, Pallas kernels, on_device(): pl.pallas_call(kernel, out_shape=jax.ShapeDtypeStruct((2, W, W), jnp.bflo...  98.2 us
    broadcast_in_dim x1, other arithmetic, on_device(): return reduced.astype(jnp.float32)[:, None]  2.84 us

profile of v2, /device:TPU:1, one launch (start us, length us, event | category | flops | bytes accessed | tf_op | source)
XLA Modules:
  0.0 101.0 jit_solution(16744607260992015391)
XLA Ops:
  0.0 98.2 %shard_map.37 = bf16[2,512,512]{2,1,0:T(8,128)(2,1)} custom-call(bf16[2,512,512]{2,1,0:T(8,128)(2,1)} %bitcast.9, bf16[2,512,512]{2,1,0:T(8,128)(2,1)} %bitcast.10, bf16[2,512,512]{2,1,0:T(8,128)(2,1)} %bitcast.11), custom_call_target="tpu_custom_call" | custom-call | tf_op jit(solution)/shard_map/pallas_call | solution.py:431
  98.2 2.8 %bitcast_convert_fusion = f32[2,1,512,512]{3,2,1,0:T(8,128)} fusion(bf16[2,512,512]{2,1,0:T(8,128)(2,1)} %shard_map.37), kind=kLoop, calls=%fused_computation | loop fusion | flops 524288 | bytes 3145728 | tf_op jit(solution)/shard_map/broadcast_in_dim | solution.py:467

commit v3 on v2

--- a/solution.py
+++ b/solution.py
@@ -9,7 +9,8 @@
 W = 512
 PIECES = 4
 PIECE = W // PIECES
-RELAYED = (3,)
+RELAYED = ((0, 3), (1, 2), (1, 3))
+BENT = (*RELAYED, (0, 2))
 L, U, F = 0, 1, 2
 COLUMNS = ((0, 256), (256, 256))
 
@@ -75,6 +76,15 @@
     goal, goal_cross = (device_at(*partner_end, end_z, c) for c in (core, 1 - core))
     origin, origin_cross = (device_at(*flip(end_chip), end_z, c) for c in (core, 1 - core))
     chain_end, chain_end_cross = (device_at(*end_chip, end_z, c) for c in (core, 1 - core))
+
+    bend = (top & (row == 7)) | (bottom & (row == 8))
+    partner_bend = (top & (partner_row == 7)) | (bottom & (partner_row == 8))
+    bend_relay = (top & (row == 14)) | (bottom & (row == 1))
+    relay_to = device_at(x, (y + jnp.where(bend, jnp.where(top, 3, 1), 2)) % 4, z, core)
+    relay_goal = choose(bend_relay, chip_of_row(jnp.where(top, 8, 7)), partner_end)
+    relay_goal = device_at(*relay_goal, end_z, core)
+    bend_sender = device_at(*chip_of_row(jnp.where(top, 7, 8)), z, core)
+    bend_source = device_at(*chip_of_row(jnp.where(top, 1, 14)), end_z, core)
     crosses = (top & (core == 1)) | (bottom & (core == 0))
 
     def copy_in(kind, source):
@@ -99,6 +109,8 @@
     greet(preceding_cross, ~bottom & (core == 0))
     greet(chain_end, has_end & lead)
     greet(origin, has_end)
+    greet(bend_sender, bend_relay)
+    greet(bend_source, bend)
     greet(origin_cross, has_end & lead & crosses)
     greet(chain_end_cross, has_end & trail & crosses)
     expected = (
@@ -107,6 +119,8 @@
         ~top & (core == 1),
         ~bottom & (core == 0),
         has_end & lead,
+        bend,
+        bend_relay,
         partner_has_end,
         partner_has_end & trail & crosses,
         has_end & trail & crosses,
@@ -179,19 +193,20 @@
     def reaches(kind, upward):
         return kind == F or (kind == U) == upward
 
-    for kind, source in kinds:
+    def start(kind):
+        source = kinds[kind][1]
         for index in range(PIECES):
             other = piece(source.at[1 - half], kind, index)
             to_mine(other, 1 + half, kind, index, in_send.at[kind, index], partner, None)
             to_mine(other, mine_end, kind, index, extra_send.at[0, kind, index], goal, lead)
-            if index in RELAYED:
+            if (kind, index) in BENT:
                 send(
                     piece(source.at[half], kind, index),
                     piece(relay.at[kind], kind, index),
                     relay_send.at[0, kind, index],
                     relay_recv.at[kind, index],
-                    partner,
-                    lead & has_end,
+                    relay_to,
+                    lead & has_end if (kind, index) in RELAYED else bend,
                 )
             for upward, side in ((True, top), (False, bottom)):
                 if reaches(kind, upward):
@@ -230,7 +245,8 @@
         to_near(part, slot + core, kind, index, twin_send.at[number, kind, index], twin)
         upward = second if local else first
         if local:
-            chain = ~lead if index in RELAYED else None
+            bent = ~bend if (kind, index) in BENT else None
+            chain = ~lead if (kind, index) in RELAYED else bent
         else:
             chain = ~trail
         for way, device, there, target in (
@@ -266,11 +282,13 @@
         arrive(part, mine_recv.at[2 - half, kind, index])
         cut(2 - half, kind, part)
         pass_on(2 - half, kind, index, False)
-        if index in RELAYED:
+        if (kind, index) in BENT:
             part = piece(relay.at[kind], kind, index)
-            waiting = trail & partner_has_end
+            waiting = bend_relay
+            if (kind, index) in RELAYED:
+                waiting |= trail & partner_has_end & ~partner_bend
             arrive(part, relay_recv.at[kind, index], waiting)
-            to_mine(part, mine_end, kind, index, relay_send.at[1, kind, index], goal, waiting)
+            to_mine(part, mine_end, kind, index, relay_send.at[1, kind, index], relay_goal, waiting)
 
     def halo(kind, index):
         for slot, there in ((0, has_prev), (3, has_next)):
@@ -334,8 +352,11 @@
 
     every = range(PIECES)
     inside = ~end
+    start(L)
     local(L)
+    start(U)
     local(U)
+    start(F)
     for kind in (L, U):
         for index in every:
             forward(kind, index)

time: 101 us -> 94 us (0.931)
  the two profiles are of different devices: /device:TPU:1 before, /device:TPU:7 now
where the time goes in v3:
time: 94 us; the launch traced here: 93.9 us
  Pallas kernels  91 us (97%)
  other arithmetic  2.84 us (3%)
    pallas_call x1, Pallas kernels, on_device(): pl.pallas_call(kernel, out_shape=jax.ShapeDtypeStruct((2, W, W), jnp.bflo...  91 us
    broadcast_in_dim x1, other arithmetic, on_device(): return reduced.astype(jnp.float32)[:, None]  2.84 us

profile of v3, /device:TPU:7, one launch (start us, length us, event | category | flops | bytes accessed | tf_op | source)
XLA Modules:
  0.0 93.9 jit_solution(10395114838917283646)
XLA Ops:
  0.0 91.0 %shard_map.37 = bf16[2,512,512]{2,1,0:T(8,128)(2,1)} custom-call(bf16[2,512,512]{2,1,0:T(8,128)(2,1)} %bitcast.9, bf16[2,512,512]{2,1,0:T(8,128)(2,1)} %bitcast.10, bf16[2,512,512]{2,1,0:T(8,128)(2,1)} %bitcast.11), custom_call_target="tpu_custom_call" | custom-call | tf_op jit(solution)/shard_map/pallas_call | solution.py:452
  91.0 2.8 %bitcast_convert_fusion = f32[2,1,512,512]{3,2,1,0:T(8,128)} fusion(bf16[2,512,512]{2,1,0:T(8,128)(2,1)} %shard_map.37), kind=kLoop, calls=%fused_computation | loop fusion | flops 524288 | bytes 3145728 | tf_op jit(solution)/shard_map/broadcast_in_dim | solution.py:488

commit v4 on v3

--- a/solution.py
+++ b/solution.py
@@ -437,12 +437,12 @@
         for slot in (0, 1):
             for index in indices:
                 send_out(slot, index)
+    for condition, copy in sent:
+        only(condition, copy.wait_send)
     for index in range(PIECES):
         for slot in (0, 1):
             pl.when(half == slot)(home_copy(slot, index).wait)
         arrive(piece(out.at[1 - half], F, index), out_recv.at[index])
-    for condition, copy in sent:
-        only(condition, copy.wait_send)
 
 
 def on_device(lower, upper, rhs):

time: 94 us -> 93.7 us (level)
  no operation moved by 1% of the time
where the time goes in v4:
time: 93.7 us; the launch traced here: 93.6 us
  Pallas kernels  90.8 us (97%)
  other arithmetic  2.84 us (3%)
    pallas_call x1, Pallas kernels, on_device(): pl.pallas_call(kernel, out_shape=jax.ShapeDtypeStruct((2, W, W), jnp.bflo...  90.8 us
    broadcast_in_dim x1, other arithmetic, on_device(): return reduced.astype(jnp.float32)[:, None]  2.84 us

profile of v4, /device:TPU:7, one launch (start us, length us, event | category | flops | bytes accessed | tf_op | source)
XLA Modules:
  0.0 93.6 jit_solution(3980248097120844935)
XLA Ops:
  0.0 90.8 %shard_map.37 = bf16[2,512,512]{2,1,0:T(8,128)(2,1)} custom-call(bf16[2,512,512]{2,1,0:T(8,128)(2,1)} %bitcast.9, bf16[2,512,512]{2,1,0:T(8,128)(2,1)} %bitcast.10, bf16[2,512,512]{2,1,0:T(8,128)(2,1)} %bitcast.11), custom_call_target="tpu_custom_call" | custom-call | tf_op jit(solution)/shard_map/pallas_call | solution.py:452
  90.8 2.8 %bitcast_convert_fusion = f32[2,1,512,512]{3,2,1,0:T(8,128)} fusion(bf16[2,512,512]{2,1,0:T(8,128)(2,1)} %shard_map.37), kind=kLoop, calls=%fused_computation | loop fusion | flops 524288 | bytes 3145728 | tf_op jit(solution)/shard_map/broadcast_in_dim | solution.py:488
